TPU v7x, 128 devices: a whole 4x4x4 slice. The times are simulated.
128 devices in a mesh: row: 8 (over y_lo, x), col: 16 (over z, y_hi, core).
Axes of the slice: x: 4, y: 4 (y_hi: 2, y_lo: 2; y = y_hi * 2 + y_lo), z: 4, core: 2. Of those that a mesh axis runs over, the one named last changes fastest.
Arguments:
- pair_rep: float32 [512, 512, 128], P('row', 'col'), may hold values from -24 to 24
- gain_start: float32 [128], replicated, may hold values from 0.5 to 1.5
- project_start: bfloat16 [128, 512], replicated, may hold values from -0.5 to 0.5
- gate_bias_start: float32 [128], replicated, may hold values from -1 to 2
- bias_start: bfloat16 [128, 4], replicated, may hold values from -18 to 18
- out_start: bfloat16 [128, 128], replicated, may hold values from -0.5 to 0.5
- gain_end: float32 [128], replicated, may hold values from 0.5 to 1.5
- project_end: bfloat16 [128, 512], replicated, may hold values from -0.5 to 0.5
- gate_bias_end: float32 [128], replicated, may hold values from -1 to 2
- bias_end: bfloat16 [128, 4], replicated, may hold values from -18 to 18
- out_end: bfloat16 [128, 128], replicated, may hold values from -0.5 to 0.5
Outputs:
- pair_out: float32 [512, 512, 128], P('row', 'col')
All inputs are finite; a program needn't handle non-finite values.
Results may differ from a plain program's by a relative error of at most 0.011.
Values may be sent and summed in bfloat16 or wider, within the bound.
A program may use at most 128 MiB of HBM per device.

v0:
```python
import jax
import jax.numpy as jnp
from jax import lax
from jax.sharding import PartitionSpec as P


def broadcast(value, axis, root):
    mine = lax.axis_index(axis) == root
    return lax.psum(jnp.where(mine, value, jnp.zeros_like(value)), axis)


def layer_norm(values, gain):
    centre_mean = jnp.mean(values, axis=-1, keepdims=True)
    centred = values - centre_mean
    variance = jnp.mean(centred * centred, axis=-1, keepdims=True)
    return (centred * lax.rsqrt(variance + 1e-05) * gain).astype(jnp.bfloat16)


def softmax_update(state_now, scores, value_rows, value_form):
    highest, normaliser, weighted = state_now
    new_high = jnp.maximum(highest, jnp.max(scores, axis=-1))
    weights_exp = jnp.exp(scores - new_high[..., None])
    normaliser = jnp.sum(weights_exp, axis=-1)
    added = jnp.einsum(
        value_form, weights_exp.astype(jnp.bfloat16), value_rows, preferred_element_type=jnp.float32
    )
    weighted = added
    return (new_high, normaliser, weighted)


def finish_section(state_now, gate_open, out_weight, tile_shape):
    weighted = state_now[2] / state_now[1][..., None]
    rows_dev, cols_dev, channels = tile_shape
    head_count, head_size = (weighted.shape[2], weighted.shape[3])
    gated = (gate_open.reshape(rows_dev, cols_dev, head_count, head_size) * weighted).astype(
        jnp.bfloat16
    )
    gated = gated.reshape(rows_dev * cols_dev, head_count * head_size)
    return jnp.dot(gated, out_weight, preferred_element_type=jnp.float32).reshape(
        rows_dev, cols_dev, channels
    )


def start_section(pair_rep, gain, project, gate_bias, bias_weight, out_weight):
    rows_dev, cols_dev, channels = pair_rep.shape
    head_count = bias_weight.shape[1]
    inner_width = out_weight.shape[0]
    head_size = inner_width // head_count
    factor = lax.axis_size("col") // lax.axis_size("row")
    score_scale = head_size ** (-0.5)
    normed = layer_norm(pair_rep, gain)
    flat_rows = normed.reshape(rows_dev * cols_dev, channels)
    projected = jnp.dot(flat_rows, project, preferred_element_type=jnp.float32)
    query_rows = (
        projected[:, :inner_width]
        .astype(jnp.bfloat16)
        .reshape(rows_dev, cols_dev, head_count, head_size)
    )
    gate_open = jax.nn.sigmoid(projected[:, 3 * inner_width :] + gate_bias)
    tile_bias = jnp.dot(flat_rows, bias_weight, preferred_element_type=jnp.float32).reshape(
        rows_dev, cols_dev, head_count
    )
    row_bias = lax.all_gather(tile_bias, "col", axis=1, tiled=True)
    column = lax.axis_index("col")
    own_rows = lax.dynamic_slice_in_dim(row_bias, column % factor * cols_dev, cols_dev, 0)
    mirrored = broadcast(own_rows, "row", column // factor)
    mirrored = jnp.transpose(mirrored, (0, 2, 1))
    initial = (
        jnp.full((rows_dev, cols_dev, head_count), -1e30, jnp.float32),
        jnp.zeros((rows_dev, cols_dev, head_count), jnp.float32),
        jnp.zeros((rows_dev, cols_dev, head_count, head_size), jnp.float32),
    )
    key_tile = (
        projected[:, inner_width : 2 * inner_width]
        .astype(jnp.bfloat16)
        .reshape(rows_dev, cols_dev, inner_width)
    )
    value_tile = (
        projected[:, 2 * inner_width : 3 * inner_width]
        .astype(jnp.bfloat16)
        .reshape(rows_dev, cols_dev, inner_width)
    )
    segment = (
        lax.all_gather(key_tile, "col", axis=1, tiled=True),
        lax.all_gather(value_tile, "col", axis=1, tiled=True),
    )
    piece_len = segment[0].shape[1]
    key_rows = segment[0].reshape(rows_dev, piece_len, head_count, head_size)
    value_rows = segment[1].reshape(rows_dev, piece_len, head_count, head_size)
    scores = (
        jnp.einsum("ijhd,ikhd->ijhk", query_rows, key_rows, preferred_element_type=jnp.float32)
        * score_scale
    )
    scores = scores + mirrored[None]
    final_state = softmax_update(initial, scores, value_rows, "ijhk,ikhd->ijhd")
    return finish_section(final_state, gate_open, out_weight, pair_rep.shape)


def end_section(pair_rep, gain, project, gate_bias, bias_weight, out_weight):
    rows_dev, cols_dev, channels = pair_rep.shape
    head_count = bias_weight.shape[1]
    inner_width = out_weight.shape[0]
    head_size = inner_width // head_count
    factor = lax.axis_size("col") // lax.axis_size("row")
    score_scale = head_size ** (-0.5)
    normed = layer_norm(pair_rep, gain)
    flat_rows = normed.reshape(rows_dev * cols_dev, channels)
    projected = jnp.dot(flat_rows, project, preferred_element_type=jnp.float32)
    query_rows = (
        projected[:, :inner_width]
        .astype(jnp.bfloat16)
        .reshape(rows_dev, cols_dev, head_count, head_size)
    )
    gate_open = jax.nn.sigmoid(projected[:, 3 * inner_width :] + gate_bias)
    tile_bias = jnp.dot(flat_rows, bias_weight, preferred_element_type=jnp.float32).reshape(
        rows_dev, cols_dev, head_count
    )
    column_bias = lax.all_gather(tile_bias, "row", axis=0, tiled=True)
    row_place = lax.axis_index("row")
    strips = [
        broadcast(column_bias, "col", row_place * factor + mirror_part)
        for mirror_part in range(factor)
    ]
    mirrored = jnp.transpose(jnp.concatenate(strips, axis=1), (1, 2, 0))
    initial = (
        jnp.full((rows_dev, cols_dev, head_count), -1e30, jnp.float32),
        jnp.zeros((rows_dev, cols_dev, head_count), jnp.float32),
        jnp.zeros((rows_dev, cols_dev, head_count, head_size), jnp.float32),
    )
    key_tile = (
        projected[:, inner_width : 2 * inner_width]
        .astype(jnp.bfloat16)
        .reshape(rows_dev, cols_dev, inner_width)
    )
    value_tile = (
        projected[:, 2 * inner_width : 3 * inner_width]
        .astype(jnp.bfloat16)
        .reshape(rows_dev, cols_dev, inner_width)
    )
    segment = (
        lax.all_gather(key_tile, "row", axis=0, tiled=True),
        lax.all_gather(value_tile, "row", axis=0, tiled=True),
    )
    piece_len = segment[0].shape[0]
    key_rows = segment[0].reshape(piece_len, cols_dev, head_count, head_size)
    value_rows = segment[1].reshape(piece_len, cols_dev, head_count, head_size)
    scores = (
        jnp.einsum("ijhd,kjhd->ijhk", query_rows, key_rows, preferred_element_type=jnp.float32)
        * score_scale
    )
    scores = scores + mirrored[:, None]
    final_state = softmax_update(initial, scores, value_rows, "ijhk,kjhd->ijhd")
    return finish_section(final_state, gate_open, out_weight, pair_rep.shape)


def local(
    pair_rep,
    gain_start,
    project_start,
    gate_bias_start,
    bias_start,
    out_start,
    gain_end,
    project_end,
    gate_bias_end,
    bias_end,
    out_end,
):
    first = pair_rep + start_section(
        pair_rep, gain_start, project_start, gate_bias_start, bias_start, out_start
    )
    return first + end_section(first, gain_end, project_end, gate_bias_end, bias_end, out_end)


def solution(mesh):
    return jax.shard_map(
        local,
        mesh=mesh,
        in_specs=(P("row", "col", None), P(), P(), P(), P(), P(), P(), P(), P(), P(), P()),
        out_specs=P("row", "col", None),
        check_vma=False,
    )
```

profile of v0, /device:TPU:16, one launch (start us, length us, event | category | flops | bytes accessed | tf_op | source)
XLA Modules:
  0.0 543.7 jit_solution(15718841295119894703)
XLA Ops:
  14.3 24.8 %all_gather.20 = f32[64,512,4]{0,2,1:T(4,128)S(1)} all-gather(f32[64,32,4]{0,2,1:T(4,128)S(1)} %copy.84), channel_id=1, replica_groups=mesh['row'=8,'col'=16] {'col'}, dimensions={1}, use_global_device_ids=true | all-gather | bytes 557056 | tf_op jit(solution)/shard_map/all_gather | solution.py:63
  48.0 3.2 reshape.112
  51.1 5.3 copy.88
  56.4 64.4 %all-reduce.4.cloned.1.call-done = f32[32,4,512]{0,1,2:T(4,128)} async-done(((f32[32,4,512]{0,1,2:T(4,128)}), f32[32,4,512]{0,1,2:T(4,128)}) %all-reduce.4.cloned.1.call-update) | async-done | bytes 262160 | tf_op jit(solution)/shard_map/psum | solution.py:9
  122.3 13.2 %all-gather.7.cloned.1.call-done = bf16[64,512,128]{2,1,0:T(8,128)(2,1)} async-done(((bf16[64,32,128]{2,1,0:T(8,128)(2,1)}), bf16[64,512,128]{2,1,0:T(8,128)(2,1)}) %all-gather.7.cloned.1.call-update) | async-done | bytes 8388624 | tf_op jit(solution)/shard_map/all_gather | solution.py:84
  135.5 11.9 %copy.81 = bf16[64,512,128]{1,2,0:T(8,128)(2,1)} copy(bf16[64,512,128]{2,1,0:T(8,128)(2,1)} %all-gather.7.cloned.1.call-done) | data formatting | bytes 16777216 | tf_op jit(solution)/shard_map/all_gather | solution.py:84
  147.4 11.7 %fusion.4 = (f32[64,32,4]{1,2,0:T(4,128)S(1)}, f32[64,4,512,32]{2,3,1,0:T(8,128)}) fusion(f32[32,4,512]{2,0,1:T(8,128)S(1)} %copy.85, bf16[64,512,4,32]{1,3,2,0:T(8,128)(2,1)} %bitcast.76, bf16[64,32,4,32]{3,2,1,0:T(4,128)(2,1)S(1)} %reshape.113), kind=kOutput, calls=%fused_computation.8 | convolution fusion | flops 281010176 | bytes 25985024 | tf_op jit(solution)/shard_map/ijhd,ikhd->ijhk/dot_general | solution.py:91
  159.4 8.0 %fusion = f32[64,32,4]{1,2,0:T(4,128)S(1)} fusion(f32[64,4,512,32]{2,3,1,0:T(8,128)} %get-tuple-element.18, f32[64,32,4]{1,2,0:T(4,128)S(1)} %copy.87, f32[32,4,512]{2,0,1:T(8,128)S(1)} %copy.85), kind=kLoop, calls=%fused_computation.4 | loop fusion | flops 16769024 | bytes 17104896 | tf_op jit(solution)/shard_map/reduce_sum | solution.py:23
  167.4 44.1 %all-gather.5.cloned.1.call-done = bf16[64,512,128]{2,1,0:T(8,128)(2,1)} async-done(((bf16[64,32,128]{2,1,0:T(8,128)(2,1)}), bf16[64,512,128]{2,1,0:T(8,128)(2,1)}) %all-gather.5.cloned.1.call-update) | async-done | bytes 8388624 | tf_op jit(solution)/shard_map/all_gather | solution.py:85
  211.6 11.9 %copy.80 = bf16[64,512,128]{1,2,0:T(8,128)(2,1)} copy(bf16[64,512,128]{2,1,0:T(8,128)(2,1)} %all-gather.5.cloned.1.call-done) | data formatting | bytes 16777216 | tf_op jit(solution)/shard_map/all_gather | solution.py:85
  223.5 12.2 %fusion.17 = bf16[64,32,4,32]{1,3,2,0:T(8,128)(2,1)S(1)} fusion(f32[64,32,4,32]{1,3,2,0:T(8,128)} %copy.88, bf16[64,512,4,32]{1,3,2,0:T(8,128)(2,1)} %bitcast.78, f32[64,4,512,32]{2,3,1,0:T(8,128)} %get-tuple-element.18, f32[64,32,4]{1,2,0:T(4,128)S(1)} %copy.87, f32[32,4,512]{2,0,1:T(8,128)S(1)} %copy.85, f32[64,32,4]{1,2,0:T(4,128)S(1)} %fusion), kind=kOutput, calls=%fused_computation.20 | convolution fusion | flops 285999104 | bytes 27066368 | tf_op jit(solution)/shard_map/ijhk,ikhd->ijhd/dot_general | solution.py:24
  238.6 31.3 %all_gather.23 = f32[512,32,4]{1,2,0:T(4,128)S(1)} all-gather(f32[64,32,4]{1,2,0:T(4,128)S(1)} %fusion.38), channel_id=1, replica_groups=mesh['row'=8,'col'=16] {'row'}, dimensions={0}, use_global_device_ids=true | all-gather | bytes 294912 | tf_op jit(solution)/shard_map/all_gather | solution.py:118
  271.9 2.7 fusion.48
  276.6 3.1 reshape.115
  282.2 4.4 reshape.114
  286.6 5.3 copy.98
  291.9 194.1 %all-reduce.6.cloned.1.call-done = (f32[512,32,4]{1,2,0:T(4,128)}, f32[512,32,4]{1,2,0:T(4,128)}) async-done(((f32[512,32,4]{1,2,0:T(4,128)}, f32[512,32,4]{1,2,0:T(4,128)}), (f32[512,32,4]{1,2,0:T(4,128)}, f32[512,32,4]{1,2,0:T(4,128)})) %all-reduce.6.cloned.1.call-update) | async-done | bytes 524304 | tf_op jit(solution)/shard_map/psum | solution.py:9
  486.0 3.1 maximum_bitcast_fusion
  491.5 7.6 %copy.92 = bf16[512,32,128]{0,2,1:T(8,128)(2,1)} copy(bf16[512,32,128]{2,1,0:T(8,128)(2,1)} %all-gather.11.cloned.1.call-done) | data formatting | bytes 8388608 | tf_op jit(solution)/shard_map/all_gather | solution.py:141
  499.1 7.3 %fusion.5 = (f32[64,32,4]{0,2,1:T(4,128)S(1)}, f32[32,4,512,64]{2,3,1,0:T(8,128)S(1)}) fusion(f32[64,4,512]{2,0,1:T(8,128)} %copy.95, bf16[512,32,4,32]{0,3,2,1:T(8,128)(2,1)} %bitcast.77, bf16[64,32,4,32]{3,2,1,0:T(4,128)(2,1)S(1)} %reshape.115), kind=kOutput, calls=%fused_computation.9 | convolution fusion | flops 281010176 | bytes 22052864 | tf_op jit(solution)/shard_map/ijhd,kjhd->ijhk/dot_general | solution.py:148
  506.5 5.7 %copy-done.2 = f32[32,4,512,64]{2,3,1,0:T(8,128)} copy-done((f32[32,4,512,64]{2,3,1,0:T(8,128)}, f32[32,4,512,64]{2,3,1,0:T(8,128)S(1)}, u32[]{:S(2)}) %copy-start.2) | copy-done | bytes 16777240
  512.1 4.5 fusion.2
  516.7 7.6 %copy.91 = bf16[512,32,128]{0,2,1:T(8,128)(2,1)} copy(bf16[512,32,128]{2,1,0:T(8,128)(2,1)} %all-gather.9.cloned.1.call-done) | data formatting | bytes 8388608 | tf_op jit(solution)/shard_map/all_gather | solution.py:142
  524.3 10.0 %fusion.21 = bf16[64,32,4,32]{0,3,2,1:T(8,128)(2,1)S(1)} fusion(f32[64,32,4,32]{0,3,2,1:T(8,128)} %copy.98, bf16[512,32,4,32]{0,3,2,1:T(8,128)(2,1)} %bitcast.81, f32[32,4,512,64]{2,3,1,0:T(8,128)} %copy-done.2, f32[64,32,4]{0,2,1:T(4,128)S(1)} %copy.97, f32[64,4,512]{2,0,1:T(8,128)S(1)} %copy-done.5, f32[64,32,4]{0,2,1:T(4,128)S(1)} %fusion.2), kind=kOutput, calls=%fused_computation.23 | convolution fusion | flops 285999104 | bytes 23134208 | tf_op jit(solution)/shard_map/ijhk,kjhd->ijhd/dot_general | solution.py:24
  (69 shorter events, 31.3 us)
Async XLA Ops:
  7.4 33.4 %copy-start = (bf16[128,512]{1,0:T(8,128)(2,1)S(1)}, bf16[128,512]{1,0:T(8,128)(2,1)}, u32[]{:S(2)}) copy-start(bf16[128,512]{1,0:T(8,128)(2,1)} %param.13) | copy-start | bytes 393220
  7.4 113.4 %all-reduce.4.cloned.1.call-start = ((), (), s32[]{:S(2)}) async-start(), calls=%async_computation.2 | async-start | bytes 2097152 | tf_op jit(solution)/shard_map/psum | solution.py:9
  39.1 7.3 %copy-start.10 = (f32[128]{0:T(128)S(1)}, f32[128]{0:T(128)}, u32[]{:S(2)}) copy-start(f32[128]{0:T(128)} %param.14) | copy-start | bytes 1540
  40.7 94.8 %all-gather.7.cloned.1.call-start = ((), (), s32[]{:S(2)}) async-start(), calls=%async_computation.1 | async-start | bytes 8912896 | tf_op jit(solution)/shard_map/all_gather | solution.py:84
  44.7 166.8 %all-gather.5.cloned.1.call-start = ((), (), s32[]{:S(2)}) async-start(), calls=%async_computation | async-start | bytes 8912896 | tf_op jit(solution)/shard_map/all_gather | solution.py:85
  45.3 440.7 %all-reduce.6.cloned.1.call-start = ((), (), s32[]{:S(2)}) async-start(), calls=%async_computation.5 | async-start | bytes 4194304 | tf_op jit(solution)/shard_map/psum | solution.py:9
  223.4 12.2 %copy-start.3 = (f32[64,32,128]{2,1,0:T(8,128)S(1)}, f32[64,32,128]{2,1,0:T(8,128)}, u32[]{:S(2)}) copy-start(f32[64,32,128]{2,1,0:T(8,128)} %param.11) | copy-start | bytes 3145732
  223.4 12.2 %copy-start.7 = (bf16[128,128]{1,0:T(8,128)(2,1)S(1)}, bf16[128,128]{1,0:T(8,128)(2,1)}, u32[]{:S(2)}) copy-start(bf16[128,128]{1,0:T(8,128)(2,1)} %param.16) | copy-start | bytes 98308
  223.4 13.8 %copy-start.11 = (f32[128]{0:T(128)S(1)}, f32[128]{0:T(128)}, u32[]{:S(2)}) copy-start(f32[128]{0:T(128)} %param.17) | copy-start | bytes 1540
  223.4 14.4 %copy-start.9 = (bf16[128,4]{0,1:T(4,128)(2,1)S(1)}, bf16[128,4]{0,1:T(4,128)(2,1)}, u32[]{:S(2)}) copy-start(bf16[128,4]{0,1:T(4,128)(2,1)} %param.20) | copy-start | bytes 3076
  235.6 36.3 %copy-start.6 = (bf16[128,512]{1,0:T(8,128)(2,1)S(1)}, bf16[128,512]{1,0:T(8,128)(2,1)}, u32[]{:S(2)}) copy-start(bf16[128,512]{1,0:T(8,128)(2,1)} %param.18) | copy-start | bytes 393220
  271.6 8.1 %copy-start.12 = (f32[128]{0:T(128)S(1)}, f32[128]{0:T(128)}, u32[]{:S(2)}) copy-start(f32[128]{0:T(128)} %param.19) | copy-start | bytes 1540
  271.7 219.8 %all-gather.11.cloned.1.call-start = ((), (), s32[]{:S(2)}) async-start(), calls=%async_computation.4 | async-start | bytes 4718592 | tf_op jit(solution)/shard_map/all_gather | solution.py:141
  275.9 240.8 %all-gather.9.cloned.1.call-start = ((), (), s32[]{:S(2)}) async-start(), calls=%async_computation.3 | async-start | bytes 4718592 | tf_op jit(solution)/shard_map/all_gather | solution.py:142
  499.1 13.1 %copy-start.4 = (f32[64,4,512]{2,0,1:T(8,128)S(1)}, f32[64,4,512]{2,0,1:T(8,128)}, u32[]{:S(2)}) copy-start(f32[64,4,512]{2,0,1:T(8,128)} %copy.95) | copy-start | bytes 1572868
  506.4 5.7 %copy-start.2 = (f32[32,4,512,64]{2,3,1,0:T(8,128)}, f32[32,4,512,64]{2,3,1,0:T(8,128)S(1)}, u32[]{:S(2)}) copy-start(f32[32,4,512,64]{2,3,1,0:T(8,128)S(1)} %get-tuple-element.24) | copy-start | bytes 50331652
  516.6 7.7 %copy-start.5 = (f32[64,4,512]{2,0,1:T(8,128)S(1)}, f32[64,4,512]{2,0,1:T(8,128)}, u32[]{:S(2)}) copy-start(f32[64,4,512]{2,0,1:T(8,128)} %copy.95) | copy-start | bytes 1572868
  524.3 10.8 %copy-start.8 = (bf16[128,128]{1,0:T(8,128)(2,1)S(1)}, bf16[128,128]{1,0:T(8,128)(2,1)}, u32[]{:S(2)}) copy-start(bf16[128,128]{1,0:T(8,128)(2,1)} %param.21) | copy-start | bytes 98308
  524.3 12.1 %copy-start.1 = (bf16[128,512]{1,0:T(8,128)(2,1)S(1)}, bf16[128,512]{1,0:T(8,128)(2,1)}, u32[]{:S(2)}) copy-start(bf16[128,512]{1,0:T(8,128)(2,1)} %param.13) | copy-start | bytes 393220
Sparse Core Ops, SparseCore 0:
  40.8 79.8 all-reduce.3
  276.0 50.9 all-gather.10
  328.7 51.3 all-gather.8
Sparse Core Ops, SparseCore 1:
  44.8 90.7 all-gather.6
  137.8 73.8 all-gather.4
  271.7 214.2 all-reduce.5
where the time goes:
time: 550 us; the launch traced here: 544 us
  waiting for transfers between devices  317 us (58%)
  local copies, waits for them, and re-layouts  74.3 us (14%)
  blocking collectives  56.1 us (10%)
  matrix products  50.9 us (9%)
  other arithmetic  29.5 us (5%)
  between operations  15.1 us (3%)
    psum x2, waiting for transfers between devices, broadcast(): return lax.psum(jnp.where(mine, value, jnp.zeros_like(value)), axis)  258 us
    all_gather x1, waiting for transfers between devices, start_section(): lax.all_gather(value_tile, 'col', axis=1, tiled=True)  44.1 us
    all_gather x1, blocking collectives, end_section(): column_bias = lax.all_gather(tile_bias, 'row', axis=0, tiled=True)  31.3 us
    all_gather x1, blocking collectives, start_section(): row_bias = lax.all_gather(tile_bias, 'col', axis=1, tiled=True)  24.8 us
    dot_general x2, matrix products, softmax_update(): jnp.einsum(value_form, weights_exp.astype(jnp.bfloat16), value_rows, pref...  22.1 us
    reshape x4, local copies, waits for them, and re-layouts, finish_section(): gate_open.reshape(rows_dev, cols_dev, head_count, head_size) * weighted  18.1 us
    all_gather x1, waiting for transfers between devices, start_section(): lax.all_gather(key_tile, 'col', axis=1, tiled=True)  13.2 us
    reduce_sum x2, other arithmetic, softmax_update(): normaliser = jnp.sum(weights_exp, axis=-1)  12.6 us
  transfers between devices with their start and end apart: 6, of which 4 were waited for; matrix products, arithmetic and copies ran while one was open for 17% of the time, Pallas kernels for 0%

commit v1 on v0

v1 whole, which is shorter than its diff:
```python
import functools

import jax
import jax.numpy as jnp
from jax import lax
from jax.experimental import pallas as pl
from jax.experimental.pallas import tpu as pltpu
from jax.sharding import PartitionSpec as P

MESH = pl.DeviceIdType.MESH
LOG2E = 1.4426950408889634
BF16 = jnp.bfloat16
F32 = jnp.float32


def layer_norm(values, gain):
    centred = values - jnp.mean(values, axis=-1, keepdims=True)
    variance = jnp.mean(centred * centred, axis=-1, keepdims=True)
    return (centred * lax.rsqrt(variance + 1e-05) * gain).astype(BF16)


def head_max(values):
    turned = values.T
    rows = turned.shape[1]
    turned = jnp.max(turned.reshape(4, 32, rows), axis=1, keepdims=True)
    return jnp.broadcast_to(turned, (4, 32, rows)).reshape(128, rows).T


def spread_weight(weight):
    head = lax.broadcasted_iota(jnp.int32, (128, 128), 1) // 32
    weight = weight.astype(F32)
    out = jnp.zeros((128, 128), F32)
    for h in range(4):
        out = jnp.where(head == h, weight[:, h : h + 1], out)
    return out.astype(BF16)


def bias_rows(normed, weight, rows):
    every = jnp.dot(normed, weight, preferred_element_type=F32) * LOG2E
    k_lane = lax.broadcasted_iota(jnp.int32, (1, 32, 128), 2) % 32
    k_row = lax.broadcasted_iota(jnp.int32, (1, 32, 128), 1)
    return jnp.sum(jnp.where(k_lane == k_row, every.reshape(rows, 32, 128), 0.0), axis=1)


def prepare(index, x, project, gate_bias, query, key, value, gate):
    projected = jnp.dot(x, project, preferred_element_type=F32)
    query[index] = (projected[:, :128] * (32**-0.5 * LOG2E)).astype(BF16)
    gate[index] = jax.nn.sigmoid(projected[:, 384:] + gate_bias)
    keys = projected[:, 128:256].astype(BF16).reshape(16, 32, 128)
    values = projected[:, 256:384].astype(BF16).reshape(16, 32, 128)
    head = lax.broadcasted_iota(jnp.int32, (1, 32, 128), 2) // 32
    for h in range(4):
        key[index, :, h] = jnp.where(head == h, keys, jnp.zeros_like(keys))
        value[index, :, h, :, :128] = jnp.where(head == h, values, jnp.zeros_like(values))


def attend(index, start, bias, query, key, value, gate, out):
    scores = lax.dot_general(
        query[index, pl.ds(start, 128)],
        key[index].reshape(2048, 128),
        (((1,), (1,)), ((), ())),
        preferred_element_type=F32,
    )
    slot = start // 32
    parts = [
        scores[:, 128 * b : 128 * (b + 1)]
        + bias[pl.ds(slot, 4), b].reshape(128, 128).astype(F32)
        for b in range(16)
    ]
    high = head_max(functools.reduce(jnp.maximum, parts))
    expo = jnp.concatenate([jnp.exp2(part - high).astype(BF16) for part in parts], axis=1)
    both = jnp.dot(expo, value[index].reshape(2048, 256), preferred_element_type=F32)
    out[index, pl.ds(start, 128)] = (
        gate[index, pl.ds(start, 128)] * (both[:, :128] / both[:, 128:])
    ).astype(BF16)


def remote(src, dst, send, recv, device):
    return pltpu.make_async_remote_copy(
        src_ref=src, dst_ref=dst, send_sem=send, recv_sem=recv, device_id=device, device_id_type=MESH
    )


def kernel(
    pair, gain_s, project_s, gate_bias_s, bias_s, out_s, gain_e, project_e, gate_bias_e, bias_e, out_e,
    result,
    normed_s, normed_e, mine_s, mine_e, line_s, line_e, whole_s, whole_e, full_s, full_e,
    query, key, value, gate, gated_s, gated_e, home_s, home_e, first,
    send_x_s, recv_x_s, send_x_e, recv_x_e, send_l_s, recv_l_s, send_l_e, recv_l_e,
    send_b_s, recv_b_s, send_b_e, recv_b_e, send_c_s, recv_c_s, send_c_e, recv_c_e,
    send_h_s, recv_h_s, send_h_e, recv_h_e,
):
    r = lax.axis_index("row")
    c = lax.axis_index("col")
    core = c % 2
    sibling = {"col": c + 1 - 2 * core}

    barrier = pltpu.get_barrier_semaphore()
    for s in range(1, 16):
        pl.semaphore_signal(barrier, inc=1, device_id={"col": (c + s) % 16}, device_id_type=MESH)
    for s in range(1, 8):
        pl.semaphore_signal(barrier, inc=1, device_id={"row": (r + s) % 8}, device_id_type=MESH)

    head = lax.broadcasted_iota(jnp.int32, (1, 32, 128), 2) // 32
    for i in range(4):
        for h in range(4):
            value[i, :, h, :, 128:] = jnp.broadcast_to(
                jnp.where(head == h, 1.0, 0.0).astype(BF16), (16, 32, 128)
            )


    def share_bias(place, slot, device_of, line, full, send_b, recv_b, send_c):
        values = line[...]
        high = head_max(jnp.max(values, axis=0))
        full[slot] = (values - high[None]).astype(BF16)
        mate = place + 1 - 2 * (place % 2)
        order = [mate]
        for t in range(1, 4):
            part = (place // 2 + 4 - t) % 4
            order += [2 * part, 2 * part + 1]
        for other in order:
            remote(
                full.at[slot], full.at[slot], send_b.at[other], recv_b.at[place], device_of(other)
            ).start()

    def attention(place, device_of, x, project, gate_bias, full, gated, send_b, recv_b, send_c, recv_c, send_home):
        def copy_to_sibling(other):
            spot = 2 * other + core
            return remote(full.at[spot], full.at[spot], send_c.at[other], recv_c.at[other], sibling)

        def from_sibling(other):
            spot = 2 * other + 1 - core
            return remote(full.at[spot], full.at[spot], send_c.at[other], recv_c.at[other], sibling)

        copy_to_sibling(place).start()

        def one_row(i, carry):
            prepare(i, x[i], project[...], gate_bias[...], query, key, value, gate)
            return carry

        lax.fori_loop(0, 4, one_row, 0)

        def chunk(t, carry):
            part = (place // 2 + t) % 4
            for u in range(2):
                other = 2 * part + u

                @pl.when(other != place)
                def _():
                    spot = 2 * other + core
                    remote(
                        full.at[spot], full.at[spot], send_b.at[other], recv_b.at[other], device_of(other)
                    ).wait_recv()
                    copy_to_sibling(other).start()

            for u in range(2):
                from_sibling(2 * part + u).wait_recv()
            start = pl.multiple_of(part * 128, 128)
            for i in range(4):
                attend(i, start, full, query, key, value, gate, gated)
            send_home(part)
            return carry

        lax.fori_loop(0, 4, chunk, 0)
        for other in range(8):
            copy_to_sibling(other).wait_send()

    weight = spread_weight(bias_s[...])

    def norm_start(t, carry):
        normed = layer_norm(pair[pl.ds(pl.multiple_of(t * 256, 256), 256)], gain_s[...])
        normed_s[pl.ds(t * 8, 8)] = normed.reshape(8, 32, 128)
        mine_s[pl.ds(pl.multiple_of(t * 8, 8), 8)] = bias_rows(normed, weight, 8)
        return carry

    lax.fori_loop(0, 8, norm_start, 0)

    pl.semaphore_wait(barrier, 22)

    def line_copy_s(s):
        p = (c + s) % 16
        return remote(
            mine_s.at[pl.ds(pl.multiple_of(32 * (p % 2), 32), 32)], line_s.at[c],
            send_l_s.at[s], recv_l_s.at[s], {"col": p},
        )

    def tile_copy_s(s):
        p = (c + s) % 16
        return remote(
            normed_s.at[pl.ds(4 * p, 4)], whole_s.at[:, pl.ds(pl.multiple_of(32 * c, 32), 32)],
            send_x_s.at[s], recv_x_s.at[s], {"col": p},
        )

    for s in range(1, 16):
        line_copy_s(s).start()
    for s in range(1, 16):
        tile_copy_s(s).start()
    line_s[c] = mine_s[pl.ds(pl.multiple_of(32 * core, 32), 32)]
    whole_s[:, pl.ds(pl.multiple_of(32 * c, 32), 32)] = normed_s[pl.ds(4 * c, 4)]
    for s in range(1, 16):
        line_copy_s(s).wait_recv()
    share_bias(r, 2 * r + core, lambda other: {"row": other}, line_s, full_s, send_b_s, recv_b_s, send_c_s)
    for s in range(1, 16):
        tile_copy_s(s).wait_recv()

    def home_copy_s(p):
        return remote(
            gated_s.at[:, pl.ds(pl.multiple_of(32 * p, 32), 32)], home_s.at[pl.ds(4 * c, 4)],
            send_h_s.at[p], recv_h_s.at[c], {"col": p},
        )

    def send_home_s(part):
        for u in range(4):
            p = 4 * part + u

            @pl.when(p != c)
            def _():
                home_copy_s(p).start()

            @pl.when(p == c)
            def _():
                home_s[pl.ds(4 * c, 4)] = gated_s[:, pl.ds(pl.multiple_of(32 * c, 32), 32)]

    attention(
        r, lambda other: {"row": other}, whole_s, project_s, gate_bias_s, full_s, gated_s,
        send_b_s, recv_b_s, send_c_s, recv_c_s, send_home_s,
    )
    for s in range(1, 16):
        p = (c + s) % 16
        remote(
            gated_s.at[:, pl.ds(0, 32)], home_s.at[pl.ds(4 * p, 4)], send_h_s.at[p], recv_h_s.at[p], {"col": p}
        ).wait_recv()

    weight_e = spread_weight(bias_e[...])

    def residual(t, carry):
        rows = pl.ds(pl.multiple_of(t * 256, 256), 256)
        update = jnp.dot(
            home_s[pl.ds(t * 8, 8)].reshape(256, 128), out_s[...], preferred_element_type=F32
        )
        first[rows] = pair[rows] + update
        return carry

    lax.fori_loop(0, 8, residual, 0)

    def norm_end(t, carry):
        values = jnp.concatenate([first[pl.ds(t * 8 + u, 64, stride=32)] for u in range(8)], axis=0)
        normed = layer_norm(values, gain_e[...])
        normed_e[pl.ds(t * 8, 8)] = normed.reshape(8, 64, 128)
        rows = bias_rows(normed, weight_e, 16).reshape(8, 2, 128)
        for b in range(2):
            mine_e[b, pl.ds(pl.multiple_of(t * 8, 8), 8)] = rows[:, b]
        return carry

    lax.fori_loop(0, 4, norm_end, 0)

    def line_copy_e(s):
        p = (r + s) % 8
        return remote(mine_e, line_e.at[pl.ds(2 * r, 2)], send_l_e.at[s], recv_l_e.at[s], {"row": p})

    def tile_copy_e(s):
        p = (r + s) % 8
        return remote(
            normed_e.at[pl.ds(4 * p, 4)], whole_e.at[:, pl.ds(pl.multiple_of(64 * r, 64), 64)],
            send_x_e.at[s], recv_x_e.at[s], {"row": p},
        )

    for s in range(1, 8):
        line_copy_e(s).start()
    for s in range(1, 8):
        tile_copy_e(s).start()
    line_e[pl.ds(2 * r, 2)] = mine_e[...]
    whole_e[:, pl.ds(pl.multiple_of(64 * r, 64), 64)] = normed_e[pl.ds(4 * r, 4)]
    for s in range(1, 8):
        line_copy_e(s).wait_recv()
    share_bias(c // 2, c, lambda other: {"col": 2 * other + core}, line_e, full_e, send_b_e, recv_b_e, send_c_e)
    for s in range(1, 8):
        tile_copy_e(s).wait_recv()

    def home_copy_e(p):
        return remote(
            gated_e.at[:, pl.ds(pl.multiple_of(64 * p, 64), 64)], home_e.at[pl.ds(4 * r, 4)],
            send_h_e.at[p], recv_h_e.at[r], {"row": p},
        )

    def send_home_e(part):
        for u in range(2):
            p = 2 * part + u

            @pl.when(p != r)
            def _():
                home_copy_e(p).start()

            @pl.when(p == r)
            def _():
                home_e[pl.ds(4 * r, 4)] = gated_e[:, pl.ds(pl.multiple_of(64 * r, 64), 64)]

    attention(
        c // 2, lambda other: {"col": 2 * other + core}, whole_e, project_e, gate_bias_e, full_e, gated_e,
        send_b_e, recv_b_e, send_c_e, recv_c_e, send_home_e,
    )
    for s in range(1, 8):
        p = (r + s) % 8
        remote(
            gated_e.at[:, pl.ds(0, 64)], home_e.at[pl.ds(4 * p, 4)], send_h_e.at[p], recv_h_e.at[p], {"row": p}
        ).wait_recv()

    def finish(t, carry):
        update = jnp.dot(
            home_e[pl.ds(t * 8, 8)].reshape(512, 128), out_e[...], preferred_element_type=F32
        )
        for u in range(8):
            rows = pl.ds(t * 8 + u, 64, stride=32)
            result[rows] = first[rows] + update[64 * u : 64 * (u + 1)]
        return carry

    lax.fori_loop(0, 4, finish, 0)

    for s in range(1, 16):
        line_copy_s(s).wait_send()
        tile_copy_s(s).wait_send()
        home_copy_s((c + s) % 16).wait_send()
    for s in range(1, 8):
        line_copy_e(s).wait_send()
        tile_copy_e(s).wait_send()
        home_copy_e((r + s) % 8).wait_send()
        other = (r + s) % 8
        remote(
            full_s.at[2 * r + core], full_s.at[2 * r + core], send_b_s.at[other], recv_b_s.at[other], {"row": other}
        ).wait_send()
        other = (c // 2 + s) % 8
        remote(
            full_e.at[c], full_e.at[c], send_b_e.at[other], recv_b_e.at[other], {"col": 2 * other + core}
        ).wait_send()


def local(pair, gain_s, project_s, gate_bias_s, bias_s, out_s, gain_e, project_e, gate_bias_e, bias_e, out_e):
    vmem = pl.BlockSpec(memory_space=pltpu.VMEM)
    dma = pltpu.SemaphoreType.DMA
    out = pl.pallas_call(
        kernel,
        out_shape=jax.ShapeDtypeStruct((2048, 128), F32),
        in_specs=[vmem] * 11,
        out_specs=vmem,
        scratch_shapes=[
            pltpu.VMEM((64, 32, 128), BF16),
            pltpu.VMEM((32, 64, 128), BF16),
            pltpu.VMEM((64, 128), F32),
            pltpu.VMEM((2, 32, 128), F32),
            pltpu.VMEM((16, 32, 128), F32),
            pltpu.VMEM((16, 32, 128), F32),
            pltpu.VMEM((4, 512, 128), BF16),
            pltpu.VMEM((4, 512, 128), BF16),
            pltpu.VMEM((16, 16, 32, 128), BF16),
            pltpu.VMEM((16, 16, 32, 128), BF16),
            pltpu.VMEM((4, 512, 128), BF16),
            pltpu.VMEM((4, 16, 4, 32, 128), BF16),
            pltpu.VMEM((4, 16, 4, 32, 256), BF16),
            pltpu.VMEM((4, 512, 128), F32),
            pltpu.VMEM((4, 512, 128), BF16),
            pltpu.VMEM((4, 512, 128), BF16),
            pltpu.VMEM((64, 32, 128), BF16),
            pltpu.VMEM((32, 64, 128), BF16),
            pltpu.VMEM((2048, 128), F32),
        ]
        + [dma((n,)) for n in (16, 16, 8, 8) * 2 + (8,) * 8 + (16, 16, 8, 8)],
        compiler_params=pltpu.CompilerParams(
            collective_id=0, has_side_effects=True, vmem_limit_bytes=56 * 2**20
        ),
    )(
        pair.reshape(2048, 128),
        gain_s.reshape(1, 128), project_s, gate_bias_s.reshape(1, 128), bias_s, out_s,
        gain_e.reshape(1, 128), project_e, gate_bias_e.reshape(1, 128), bias_e, out_e,
    )
    return out.reshape(pair.shape)


def solution(mesh):
    return jax.shard_map(
        local,
        mesh=mesh,
        in_specs=(P("row", "col", None), P(), P(), P(), P(), P(), P(), P(), P(), P(), P()),
        out_specs=P("row", "col", None),
        check_vma=False,
    )
```

time: 550 us -> 96.2 us (0.17)
  the two profiles are of different devices: /device:TPU:16 before, /device:TPU:105 now
where the time goes in v1:
time: 96.2 us; the launch traced here: 96 us
  Pallas kernels  91.6 us (95%)
  local copies, waits for them, and re-layouts  4.41 us (5%)
    pallas_call x1, Pallas kernels, local(): pl.pallas_call(kernel, out_shape=jax.ShapeDtypeStruct((2048, 128), F32),...  91.6 us
    unnamed x7, local copies, waits for them, and re-layouts  4.41 us

profile of v1, /device:TPU:105, one launch (start us, length us, event | category | flops | bytes accessed | tf_op | source)
XLA Modules:
  0.0 96.0 jit_solution(829783281393425380)
XLA Ops:
  0.0 0.0 copy-start
  0.0 0.7 copy-done
  0.7 0.0 copy-start.1
  0.7 0.7 copy.12.bias_s
  1.4 0.0 copy-done.1
  1.4 0.7 copy.13.bias_e
  2.1 91.6 %shard_map.109 = f32[2048,128]{1,0:T(8,128)} custom-call(f32[2048,128]{1,0:T(8,128)} %bitcast.7, f32[1,128]{1,0:T(1,128)} %bitcast.8, bf16[128,512]{1,0:T(8,128)(2,1)} %project_s.1, f32[1,128]{1,0:T(1,128)} %bitcast.9, bf16[128,4]{1,0:T(8,128)(2,1)} %copy.12.bias_s, bf16[128,128]{1,0:T(8,128)(2,1)} %out_s.1, f32[1,128]{1,0:T(1,128)} %bitcast.10, ...), custom_call_target="tpu_custom_call" | custom-call | tf_op jit(solution)/shard_map/pallas_call | solution.py:340
  93.8 2.3 %copy.15 = f32[64,32,128]{2,1,0:T(8,128)} copy(f32[64,32,128]{2,1,0:T(8,128)} %bitcast.6) | data formatting | bytes 2097152
Async XLA Ops:
  0.0 0.7 copy-start
  0.7 0.7 copy-start.1

commit v2 on v1

--- a/solution.py
+++ b/solution.py
@@ -27,16 +27,21 @@
 
 
 def spread_weight(weight):
-    head = lax.broadcasted_iota(jnp.int32, (128, 128), 1) // 32
+    head = lax.broadcasted_iota(jnp.int32, (128, 128), 0) // 32
     weight = weight.astype(F32)
     out = jnp.zeros((128, 128), F32)
     for h in range(4):
-        out = jnp.where(head == h, weight[:, h : h + 1], out)
+        out = jnp.where(head == h, weight[h : h + 1], out)
     return out.astype(BF16)
 
 
+def bias_all(normed, weight):
+    dims = (((1,), (1,)), ((), ()))
+    return lax.dot_general(normed, weight, dims, preferred_element_type=F32) * LOG2E
+
+
 def bias_rows(normed, weight, rows):
-    every = jnp.dot(normed, weight, preferred_element_type=F32) * LOG2E
+    every = bias_all(normed, weight)
     k_lane = lax.broadcasted_iota(jnp.int32, (1, 32, 128), 2) % 32
     k_row = lax.broadcasted_iota(jnp.int32, (1, 32, 128), 1)
     return jnp.sum(jnp.where(k_lane == k_row, every.reshape(rows, 32, 128), 0.0), axis=1)
@@ -75,6 +80,11 @@
     ).astype(BF16)
 
 
+def shift_bias(line, full, slot):
+    values = line[...]
+    full[slot] = (values - head_max(jnp.max(values, axis=0))[None]).astype(BF16)
+
+
 def remote(src, dst, send, recv, device):
     return pltpu.make_async_remote_copy(
         src_ref=src, dst_ref=dst, send_sem=send, recv_sem=recv, device_id=device, device_id_type=MESH
@@ -85,7 +95,7 @@
     pair, gain_s, project_s, gate_bias_s, bias_s, out_s, gain_e, project_e, gate_bias_e, bias_e, out_e,
     result,
     normed_s, normed_e, mine_s, mine_e, line_s, line_e, whole_s, whole_e, full_s, full_e,
-    query, key, value, gate, gated_s, gated_e, home_s, home_e, first,
+    query, key, value, gate, gated_s, gated_e, home_s, home_e, first, swap,
     send_x_s, recv_x_s, send_x_e, recv_x_e, send_l_s, recv_l_s, send_l_e, recv_l_e,
     send_b_s, recv_b_s, send_b_e, recv_b_e, send_c_s, recv_c_s, send_c_e, recv_c_e,
     send_h_s, recv_h_s, send_h_e, recv_h_e,
@@ -101,6 +111,7 @@
     for s in range(1, 8):
         pl.semaphore_signal(barrier, inc=1, device_id={"row": (r + s) % 8}, device_id_type=MESH)
 
+    mine_e[...] = jnp.zeros_like(mine_e)
     head = lax.broadcasted_iota(jnp.int32, (1, 32, 128), 2) // 32
     for i in range(4):
         for h in range(4):
@@ -109,21 +120,21 @@
             )
 
 
-    def share_bias(place, slot, device_of, line, full, send_b, recv_b, send_c):
-        values = line[...]
-        high = head_max(jnp.max(values, axis=0))
-        full[slot] = (values - high[None]).astype(BF16)
-        mate = place + 1 - 2 * (place % 2)
-        order = [mate]
-        for t in range(1, 4):
-            part = (place // 2 + 4 - t) % 4
-            order += [2 * part, 2 * part + 1]
-        for other in order:
+    def turn(t, lane):
+        return 0 if t == 0 else 1 + (t - 1 + lane) % 3
+
+    def send_bias(t, place, lane, slot, device_of, full, send_b, recv_b):
+        if t == 0:
+            others = [place + 1 - 2 * (place % 2)]
+        else:
+            part = (place // 2 + 4 - turn(t, lane)) % 4
+            others = [2 * part, 2 * part + 1]
+        for other in others:
             remote(
                 full.at[slot], full.at[slot], send_b.at[other], recv_b.at[place], device_of(other)
             ).start()
 
-    def attention(place, device_of, x, project, gate_bias, full, gated, send_b, recv_b, send_c, recv_c, send_home):
+    def attention(place, lane, device_of, x, project, gate_bias, full, gated, send_b, recv_b, send_c, recv_c, send_home, ready):
         def copy_to_sibling(other):
             spot = 2 * other + core
             return remote(full.at[spot], full.at[spot], send_c.at[other], recv_c.at[other], sibling)
@@ -132,29 +143,35 @@
             spot = 2 * other + 1 - core
             return remote(full.at[spot], full.at[spot], send_c.at[other], recv_c.at[other], sibling)
 
+        def pass_on(other):
+            spot = 2 * other + core
+            remote(
+                full.at[spot], full.at[spot], send_b.at[other], recv_b.at[other], device_of(other)
+            ).wait_recv()
+            copy_to_sibling(other).start()
+
         copy_to_sibling(place).start()
+        ready()
 
         def one_row(i, carry):
             prepare(i, x[i], project[...], gate_bias[...], query, key, value, gate)
             return carry
 
         lax.fori_loop(0, 4, one_row, 0)
+        pass_on(place + 1 - 2 * (place % 2))
 
         def chunk(t, carry):
-            part = (place // 2 + t) % 4
-            for u in range(2):
-                other = 2 * part + u
-
-                @pl.when(other != place)
-                def _():
-                    spot = 2 * other + core
-                    remote(
-                        full.at[spot], full.at[spot], send_b.at[other], recv_b.at[other], device_of(other)
-                    ).wait_recv()
-                    copy_to_sibling(other).start()
-
+            step = 1 - (3 - t) // 3
+            part = (place // 2 + step * (1 + (t + 2 + lane) % 3)) % 4
+            after = (place // 2 + 1 + (t + lane) % 3) % 4
             for u in range(2):
                 from_sibling(2 * part + u).wait_recv()
+
+            @pl.when(t < 3)
+            def _():
+                for u in range(2):
+                    pass_on(2 * after + u)
+
             start = pl.multiple_of(part * 128, 128)
             for i in range(4):
                 attend(i, start, full, query, key, value, gate, gated)
@@ -199,9 +216,13 @@
     whole_s[:, pl.ds(pl.multiple_of(32 * c, 32), 32)] = normed_s[pl.ds(4 * c, 4)]
     for s in range(1, 16):
         line_copy_s(s).wait_recv()
-    share_bias(r, 2 * r + core, lambda other: {"row": other}, line_s, full_s, send_b_s, recv_b_s, send_c_s)
-    for s in range(1, 16):
-        tile_copy_s(s).wait_recv()
+    shift_bias(line_s, full_s, 2 * r + core)
+    for t in range(4):
+        send_bias(t, r, c // 4, 2 * r + core, lambda other: {"row": other}, full_s, send_b_s, recv_b_s)
+
+    def ready_s():
+        for s in range(1, 16):
+            tile_copy_s(s).wait_recv()
 
     def home_copy_s(p):
         return remote(
@@ -222,37 +243,43 @@
                 home_s[pl.ds(4 * c, 4)] = gated_s[:, pl.ds(pl.multiple_of(32 * c, 32), 32)]
 
     attention(
-        r, lambda other: {"row": other}, whole_s, project_s, gate_bias_s, full_s, gated_s,
-        send_b_s, recv_b_s, send_c_s, recv_c_s, send_home_s,
-    )
-    for s in range(1, 16):
-        p = (c + s) % 16
-        remote(
-            gated_s.at[:, pl.ds(0, 32)], home_s.at[pl.ds(4 * p, 4)], send_h_s.at[p], recv_h_s.at[p], {"col": p}
-        ).wait_recv()
+        r, c // 4, lambda other: {"row": other}, whole_s, project_s, gate_bias_s, full_s, gated_s,
+        send_b_s, recv_b_s, send_c_s, recv_c_s, send_home_s, ready_s,
+    )
 
     weight_e = spread_weight(bias_e[...])
-
-    def residual(t, carry):
-        rows = pl.ds(pl.multiple_of(t * 256, 256), 256)
+    late_s = (c // 4 + 4 - r // 2) % 4
+    lane = lax.broadcasted_iota(jnp.int32, (32, 128), 1) % 32
+
+    def residual(e, carry):
+        part = (e // 3) * 3 + (1 - e // 3) * ((late_s + 5 - e) % 3)
+        for u in range(4):
+            p = 4 * part + u
+
+            @pl.when(p != c)
+            def _():
+                remote(
+                    gated_s.at[:, pl.ds(0, 32)], home_s.at[pl.ds(4 * p, 4)],
+                    send_h_s.at[p], recv_h_s.at[p], {"col": p},
+                ).wait_recv()
+
+        rows = pl.ds(pl.multiple_of(part * 512, 512), 512)
         update = jnp.dot(
-            home_s[pl.ds(t * 8, 8)].reshape(256, 128), out_s[...], preferred_element_type=F32
-        )
-        first[rows] = pair[rows] + update
+            home_s[pl.ds(part * 16, 16)].reshape(512, 128), out_s[...], preferred_element_type=F32
+        )
+        total = pair[rows] + update
+        first[rows] = total
+        normed = layer_norm(total, gain_e[...])
+        swap[rows] = normed.astype(F32)
+        every = bias_all(normed, weight_e).reshape(16, 32, 128)
+        here = lane - 16 * (part % 2)
+        mixed = mine_e[part // 2]
+        for u in range(16):
+            mixed = jnp.where(here == u, every[u], mixed)
+        mine_e[part // 2] = mixed
         return carry
 
-    lax.fori_loop(0, 8, residual, 0)
-
-    def norm_end(t, carry):
-        values = jnp.concatenate([first[pl.ds(t * 8 + u, 64, stride=32)] for u in range(8)], axis=0)
-        normed = layer_norm(values, gain_e[...])
-        normed_e[pl.ds(t * 8, 8)] = normed.reshape(8, 64, 128)
-        rows = bias_rows(normed, weight_e, 16).reshape(8, 2, 128)
-        for b in range(2):
-            mine_e[b, pl.ds(pl.multiple_of(t * 8, 8), 8)] = rows[:, b]
-        return carry
-
-    lax.fori_loop(0, 4, norm_end, 0)
+    lax.fori_loop(0, 4, residual, 0)
 
     def line_copy_e(s):
         p = (r + s) % 8
@@ -267,15 +294,26 @@
 
     for s in range(1, 8):
         line_copy_e(s).start()
+
+    def turned(t, carry):
+        for u in range(8):
+            normed_e[t * 8 + u] = swap[pl.ds(t * 8 + u, 64, stride=32)].astype(BF16)
+        return carry
+
+    lax.fori_loop(0, 4, turned, 0)
     for s in range(1, 8):
         tile_copy_e(s).start()
     line_e[pl.ds(2 * r, 2)] = mine_e[...]
     whole_e[:, pl.ds(pl.multiple_of(64 * r, 64), 64)] = normed_e[pl.ds(4 * r, 4)]
     for s in range(1, 8):
         line_copy_e(s).wait_recv()
-    share_bias(c // 2, c, lambda other: {"col": 2 * other + core}, line_e, full_e, send_b_e, recv_b_e, send_c_e)
-    for s in range(1, 8):
-        tile_copy_e(s).wait_recv()
+    shift_bias(line_e, full_e, c)
+    for t in range(4):
+        send_bias(t, c // 2, r // 2, c, lambda other: {"col": 2 * other + core}, full_e, send_b_e, recv_b_e)
+
+    def ready_e():
+        for s in range(1, 8):
+            tile_copy_e(s).wait_recv()
 
     def home_copy_e(p):
         return remote(
@@ -296,21 +334,28 @@
                 home_e[pl.ds(4 * r, 4)] = gated_e[:, pl.ds(pl.multiple_of(64 * r, 64), 64)]
 
     attention(
-        c // 2, lambda other: {"col": 2 * other + core}, whole_e, project_e, gate_bias_e, full_e, gated_e,
-        send_b_e, recv_b_e, send_c_e, recv_c_e, send_home_e,
-    )
-    for s in range(1, 8):
-        p = (r + s) % 8
-        remote(
-            gated_e.at[:, pl.ds(0, 64)], home_e.at[pl.ds(4 * p, 4)], send_h_e.at[p], recv_h_e.at[p], {"row": p}
-        ).wait_recv()
-
-    def finish(t, carry):
+        c // 2, r // 2, lambda other: {"col": 2 * other + core}, whole_e, project_e, gate_bias_e, full_e, gated_e,
+        send_b_e, recv_b_e, send_c_e, recv_c_e, send_home_e, ready_e,
+    )
+    late_e = (r // 2 + 4 - c // 4) % 4
+
+    def finish(e, carry):
+        part = (e // 3) * 3 + (1 - e // 3) * ((late_e + 5 - e) % 3)
+        for u in range(2):
+            p = 2 * part + u
+
+            @pl.when(p != r)
+            def _():
+                remote(
+                    gated_e.at[:, pl.ds(0, 64)], home_e.at[pl.ds(4 * p, 4)],
+                    send_h_e.at[p], recv_h_e.at[p], {"row": p},
+                ).wait_recv()
+
         update = jnp.dot(
-            home_e[pl.ds(t * 8, 8)].reshape(512, 128), out_e[...], preferred_element_type=F32
+            home_e[pl.ds(part * 8, 8)].reshape(512, 128), out_e[...], preferred_element_type=F32
         )
         for u in range(8):
-            rows = pl.ds(t * 8 + u, 64, stride=32)
+            rows = pl.ds(part * 8 + u, 64, stride=32)
             result[rows] = first[rows] + update[64 * u : 64 * (u + 1)]
         return carry
 
@@ -362,6 +407,7 @@
             pltpu.VMEM((64, 32, 128), BF16),
             pltpu.VMEM((32, 64, 128), BF16),
             pltpu.VMEM((2048, 128), F32),
+            pltpu.VMEM((2048, 128), F32),
         ]
         + [dma((n,)) for n in (16, 16, 8, 8) * 2 + (8,) * 8 + (16, 16, 8, 8)],
         compiler_params=pltpu.CompilerParams(
@@ -369,8 +415,8 @@
         ),
     )(
         pair.reshape(2048, 128),
-        gain_s.reshape(1, 128), project_s, gate_bias_s.reshape(1, 128), bias_s, out_s,
-        gain_e.reshape(1, 128), project_e, gate_bias_e.reshape(1, 128), bias_e, out_e,
+        gain_s.reshape(1, 128), project_s, gate_bias_s.reshape(1, 128), bias_s.T, out_s,
+        gain_e.reshape(1, 128), project_e, gate_bias_e.reshape(1, 128), bias_e.T, out_e,
     )
     return out.reshape(pair.shape)
 

time: 96.2 us -> 84.4 us (0.88)
  the two profiles are of different devices: /device:TPU:105 before, /device:TPU:65 now
where the time goes in v2:
time: 84.4 us; the launch traced here: 84.3 us
  Pallas kernels  82 us (97%)
  local copies, waits for them, and re-layouts  2.26 us (3%)
    pallas_call x1, Pallas kernels, local(): pl.pallas_call(kernel, out_shape=jax.ShapeDtypeStruct((2048, 128), F32),...  82 us
    unnamed x1, local copies, waits for them, and re-layouts  2.26 us

profile of v2, /device:TPU:65, one launch (start us, length us, event | category | flops | bytes accessed | tf_op | source)
XLA Modules:
  0.0 84.3 jit_solution(17705513973815195312)
XLA Ops:
  0.0 82.0 %shard_map.109 = f32[2048,128]{1,0:T(8,128)} custom-call(f32[2048,128]{1,0:T(8,128)} %bitcast.9, f32[1,128]{1,0:T(1,128)} %bitcast.12, bf16[128,512]{1,0:T(8,128)(2,1)} %project_s.1, f32[1,128]{1,0:T(1,128)} %bitcast.13, bf16[4,128]{1,0:T(4,128)(2,1)} %bitcast.10, bf16[128,128]{1,0:T(8,128)(2,1)} %out_s.1, f32[1,128]{1,0:T(1,128)} %bitcast.14, ...), custom_call_target="tpu_custom_call" | custom-call | tf_op jit(solution)/shard_map/pallas_call | solution.py:385
  82.0 2.3 %copy.13 = f32[64,32,128]{2,1,0:T(8,128)} copy(f32[64,32,128]{2,1,0:T(8,128)} %bitcast.8) | data formatting | bytes 2097152

commit v3 on v2

--- a/solution.py
+++ b/solution.py
@@ -59,25 +59,24 @@
         value[index, :, h, :, :128] = jnp.where(head == h, values, jnp.zeros_like(values))
 
 
-def attend(index, start, bias, query, key, value, gate, out):
+def attend(index, pair, bias, query, key, value, gate, out):
+    rows = [pl.ds(pl.multiple_of(64 * place, 64), 64) for place in pair]
     scores = lax.dot_general(
-        query[index, pl.ds(start, 128)],
+        jnp.concatenate([query[index, at] for at in rows], axis=0),
         key[index].reshape(2048, 128),
         (((1,), (1,)), ((), ())),
         preferred_element_type=F32,
     )
-    slot = start // 32
-    parts = [
-        scores[:, 128 * b : 128 * (b + 1)]
-        + bias[pl.ds(slot, 4), b].reshape(128, 128).astype(F32)
-        for b in range(16)
-    ]
+    parts = []
+    for b in range(16):
+        added = [bias[pl.ds(2 * place, 2), b].reshape(64, 128) for place in pair]
+        parts.append(scores[:, 128 * b : 128 * (b + 1)] + jnp.concatenate(added, axis=0).astype(F32))
     high = head_max(functools.reduce(jnp.maximum, parts))
     expo = jnp.concatenate([jnp.exp2(part - high).astype(BF16) for part in parts], axis=1)
     both = jnp.dot(expo, value[index].reshape(2048, 256), preferred_element_type=F32)
-    out[index, pl.ds(start, 128)] = (
-        gate[index, pl.ds(start, 128)] * (both[:, :128] / both[:, 128:])
-    ).astype(BF16)
+    mean = both[:, :128] / both[:, 128:]
+    for u, at in enumerate(rows):
+        out[index, at] = (gate[index, at] * mean[64 * u : 64 * (u + 1)]).astype(BF16)
 
 
 def shift_bias(line, full, slot):
@@ -104,12 +103,18 @@
     c = lax.axis_index("col")
     core = c % 2
     sibling = {"col": c + 1 - 2 * core}
+    x, y_lo = r % 4, r // 4
+    z, y_hi = c // 4, (c // 2) % 2
+
+    across = {"row": 4 * (1 - y_lo) + x, "col": 4 * z + 2 * (1 - y_hi) + core}
+    above = {"row": 4 * (1 - y_lo) + x, "col": 4 * z + 2 * ((y_hi + y_lo) % 2) + core}
 
     barrier = pltpu.get_barrier_semaphore()
     for s in range(1, 16):
         pl.semaphore_signal(barrier, inc=1, device_id={"col": (c + s) % 16}, device_id_type=MESH)
     for s in range(1, 8):
         pl.semaphore_signal(barrier, inc=1, device_id={"row": (r + s) % 8}, device_id_type=MESH)
+    pl.semaphore_signal(barrier, inc=1, device_id=across, device_id_type=MESH)
 
     mine_e[...] = jnp.zeros_like(mine_e)
     head = lax.broadcasted_iota(jnp.int32, (1, 32, 128), 2) // 32
@@ -120,67 +125,71 @@
             )
 
 
-    def turn(t, lane):
-        return 0 if t == 0 else 1 + (t - 1 + lane) % 3
-
-    def send_bias(t, place, lane, slot, device_of, full, send_b, recv_b):
-        if t == 0:
-            others = [place + 1 - 2 * (place % 2)]
-        else:
-            part = (place // 2 + 4 - turn(t, lane)) % 4
-            others = [2 * part, 2 * part + 1]
+    def attention(ring, line, whole, project, gate_bias, full, gated, sems, ready, send_home):
+        a, b, lane, index, device_of, mate = ring
+        send_b, recv_b, send_c, recv_c = sems
+        others = (a + 1 - 2 * (a % 2), 3 - a, (a + 2) % 4)
+        own, far = index(a, b), index(a, 1 - b)
+
+        def bias_copy(place, send, device):
+            spot = 2 * place + core
+            return remote(full.at[spot], full.at[spot], send_b.at[send], recv_b.at[place], device)
+
+        def copy_to_sibling(place):
+            spot = 2 * place + core
+            return remote(full.at[spot], full.at[spot], send_c.at[place], recv_c.at[place], sibling)
+
+        def from_sibling(place):
+            spot = 2 * place + 1 - core
+            return remote(full.at[spot], full.at[spot], send_c.at[place], recv_c.at[place], sibling)
+
+        def pass_on(place):
+            bias_copy(place, 0, mate).wait_recv()
+            copy_to_sibling(place).start()
+
+        shift_bias(line, full, 2 * own + core)
+        bias_copy(own, 0, mate).start()
+        for k, other in enumerate(others):
+            bias_copy(own, 1 + k, device_of(other)).start()
+        copy_to_sibling(own).start()
+        pass_on(far)
+        for k, other in enumerate(others):
+            bias_copy(far, 4 + k, device_of(other)).start()
+        ready()
+
+        def one_row(i, carry):
+            prepare(i, whole[i], project[...], gate_bias[...], query, key, value, gate)
+            return carry
+
+        lax.fori_loop(0, 4, one_row, 0)
         for other in others:
-            remote(
-                full.at[slot], full.at[slot], send_b.at[other], recv_b.at[place], device_of(other)
-            ).start()
-
-    def attention(place, lane, device_of, x, project, gate_bias, full, gated, send_b, recv_b, send_c, recv_c, send_home, ready):
-        def copy_to_sibling(other):
-            spot = 2 * other + core
-            return remote(full.at[spot], full.at[spot], send_c.at[other], recv_c.at[other], sibling)
-
-        def from_sibling(other):
-            spot = 2 * other + 1 - core
-            return remote(full.at[spot], full.at[spot], send_c.at[other], recv_c.at[other], sibling)
-
-        def pass_on(other):
-            spot = 2 * other + core
-            remote(
-                full.at[spot], full.at[spot], send_b.at[other], recv_b.at[other], device_of(other)
-            ).wait_recv()
-            copy_to_sibling(other).start()
-
-        copy_to_sibling(place).start()
-        ready()
-
-        def one_row(i, carry):
-            prepare(i, x[i], project[...], gate_bias[...], query, key, value, gate)
+            pass_on(index(other, b))
+
+        def chunk(t, carry):
+            half = (a // 2 + t + lane) % 2
+            side = (b + t // 2) % 2
+            pair = (index(2 * half, side), index(2 * half + 1, side))
+            for place in pair:
+                from_sibling(place).wait_recv()
+            for i in range(4):
+                attend(i, pair, full, query, key, value, gate, gated)
+            for place in pair:
+                send_home(place)
+
+            @pl.when(t == 1)
+            def _():
+                for other in others:
+                    pass_on(index(other, 1 - b))
+
             return carry
 
-        lax.fori_loop(0, 4, one_row, 0)
-        pass_on(place + 1 - 2 * (place % 2))
-
-        def chunk(t, carry):
-            step = 1 - (3 - t) // 3
-            part = (place // 2 + step * (1 + (t + 2 + lane) % 3)) % 4
-            after = (place // 2 + 1 + (t + lane) % 3) % 4
-            for u in range(2):
-                from_sibling(2 * part + u).wait_recv()
-
-            @pl.when(t < 3)
-            def _():
-                for u in range(2):
-                    pass_on(2 * after + u)
-
-            start = pl.multiple_of(part * 128, 128)
-            for i in range(4):
-                attend(i, start, full, query, key, value, gate, gated)
-            send_home(part)
-            return carry
-
         lax.fori_loop(0, 4, chunk, 0)
-        for other in range(8):
-            copy_to_sibling(other).wait_send()
+        bias_copy(own, 0, mate).wait_send()
+        for k, other in enumerate(others):
+            bias_copy(own, 1 + k, device_of(other)).wait_send()
+            bias_copy(far, 4 + k, device_of(other)).wait_send()
+        for place in range(8):
+            copy_to_sibling(place).wait_send()
 
     weight = spread_weight(bias_s[...])
 
@@ -192,7 +201,7 @@
 
     lax.fori_loop(0, 8, norm_start, 0)
 
-    pl.semaphore_wait(barrier, 22)
+    pl.semaphore_wait(barrier, 23)
 
     def line_copy_s(s):
         p = (c + s) % 16
@@ -216,9 +225,6 @@
     whole_s[:, pl.ds(pl.multiple_of(32 * c, 32), 32)] = normed_s[pl.ds(4 * c, 4)]
     for s in range(1, 16):
         line_copy_s(s).wait_recv()
-    shift_bias(line_s, full_s, 2 * r + core)
-    for t in range(4):
-        send_bias(t, r, c // 4, 2 * r + core, lambda other: {"row": other}, full_s, send_b_s, recv_b_s)
 
     def ready_s():
         for s in range(1, 16):
@@ -230,9 +236,9 @@
             send_h_s.at[p], recv_h_s.at[c], {"col": p},
         )
 
-    def send_home_s(part):
-        for u in range(4):
-            p = 4 * part + u
+    def send_home_s(place):
+        for u in range(2):
+            p = 2 * place + u
 
             @pl.when(p != c)
             def _():
@@ -242,17 +248,18 @@
             def _():
                 home_s[pl.ds(4 * c, 4)] = gated_s[:, pl.ds(pl.multiple_of(32 * c, 32), 32)]
 
+    ring_s = (x, y_lo, z, lambda a, b: 4 * b + a, lambda a: {"row": 4 * y_lo + a}, above)
     attention(
-        r, c // 4, lambda other: {"row": other}, whole_s, project_s, gate_bias_s, full_s, gated_s,
-        send_b_s, recv_b_s, send_c_s, recv_c_s, send_home_s, ready_s,
+        ring_s, line_s, whole_s, project_s, gate_bias_s, full_s, gated_s,
+        (send_b_s, recv_b_s, send_c_s, recv_c_s), ready_s, send_home_s,
     )
 
     weight_e = spread_weight(bias_e[...])
-    late_s = (c // 4 + 4 - r // 2) % 4
+    late_s = ((c // 4) % 2 + x // 2) % 2
     lane = lax.broadcasted_iota(jnp.int32, (32, 128), 1) % 32
 
     def residual(e, carry):
-        part = (e // 3) * 3 + (1 - e // 3) * ((late_s + 5 - e) % 3)
+        part = (late_s + e // 2) % 2 + 2 * (e % 2)
         for u in range(4):
             p = 4 * part + u
 
@@ -307,9 +314,6 @@
     whole_e[:, pl.ds(pl.multiple_of(64 * r, 64), 64)] = normed_e[pl.ds(4 * r, 4)]
     for s in range(1, 8):
         line_copy_e(s).wait_recv()
-    shift_bias(line_e, full_e, c)
-    for t in range(4):
-        send_bias(t, c // 2, r // 2, c, lambda other: {"col": 2 * other + core}, full_e, send_b_e, recv_b_e)
 
     def ready_e():
         for s in range(1, 8):
@@ -321,26 +325,25 @@
             send_h_e.at[p], recv_h_e.at[r], {"row": p},
         )
 
-    def send_home_e(part):
-        for u in range(2):
-            p = 2 * part + u
-
-            @pl.when(p != r)
-            def _():
-                home_copy_e(p).start()
-
-            @pl.when(p == r)
-            def _():
-                home_e[pl.ds(4 * r, 4)] = gated_e[:, pl.ds(pl.multiple_of(64 * r, 64), 64)]
-
+    def send_home_e(p):
+        @pl.when(p != r)
+        def _():
+            home_copy_e(p).start()
+
+        @pl.when(p == r)
+        def _():
+            home_e[pl.ds(4 * r, 4)] = gated_e[:, pl.ds(pl.multiple_of(64 * r, 64), 64)]
+
+    ring_e = (z, y_hi, r // 2, lambda a, b: 2 * a + b, lambda a: {"col": 4 * a + 2 * y_hi + core}, across)
     attention(
-        c // 2, r // 2, lambda other: {"col": 2 * other + core}, whole_e, project_e, gate_bias_e, full_e, gated_e,
-        send_b_e, recv_b_e, send_c_e, recv_c_e, send_home_e, ready_e,
-    )
-    late_e = (r // 2 + 4 - c // 4) % 4
+        ring_e, line_e, whole_e, project_e, gate_bias_e, full_e, gated_e,
+        (send_b_e, recv_b_e, send_c_e, recv_c_e), ready_e, send_home_e,
+    )
+
+    late_e = (y_lo + z // 2) % 2
 
     def finish(e, carry):
-        part = (e // 3) * 3 + (1 - e // 3) * ((late_e + 5 - e) % 3)
+        part = (late_e + e // 2) % 2 + 2 * (e % 2)
         for u in range(2):
             p = 2 * part + u
 
@@ -369,14 +372,6 @@
         line_copy_e(s).wait_send()
         tile_copy_e(s).wait_send()
         home_copy_e((r + s) % 8).wait_send()
-        other = (r + s) % 8
-        remote(
-            full_s.at[2 * r + core], full_s.at[2 * r + core], send_b_s.at[other], recv_b_s.at[other], {"row": other}
-        ).wait_send()
-        other = (c // 2 + s) % 8
-        remote(
-            full_e.at[c], full_e.at[c], send_b_e.at[other], recv_b_e.at[other], {"col": 2 * other + core}
-        ).wait_send()
 
 
 def local(pair, gain_s, project_s, gate_bias_s, bias_s, out_s, gain_e, project_e, gate_bias_e, bias_e, out_e):

time: 84.4 us -> 80.1 us (0.949)
  the two profiles are of different devices: /device:TPU:65 before, /device:TPU:16 now
where the time goes in v3:
time: 80.1 us; the launch traced here: 80 us
  Pallas kernels  77.7 us (97%)
  local copies, waits for them, and re-layouts  2.26 us (3%)
    pallas_call x1, Pallas kernels, local(): pl.pallas_call(kernel, out_shape=jax.ShapeDtypeStruct((2048, 128), F32),...  77.7 us
    unnamed x1, local copies, waits for them, and re-layouts  2.26 us

profile of v3, /device:TPU:16, one launch (start us, length us, event | category | flops | bytes accessed | tf_op | source)
XLA Modules:
  0.0 80.0 jit_solution(13830011727096885454)
XLA Ops:
  0.0 77.7 %shard_map.109 = f32[2048,128]{1,0:T(8,128)} custom-call(f32[2048,128]{1,0:T(8,128)} %bitcast.9, f32[1,128]{1,0:T(1,128)} %bitcast.12, bf16[128,512]{1,0:T(8,128)(2,1)} %project_s.1, f32[1,128]{1,0:T(1,128)} %bitcast.13, bf16[4,128]{1,0:T(4,128)(2,1)} %bitcast.10, bf16[128,128]{1,0:T(8,128)(2,1)} %out_s.1, f32[1,128]{1,0:T(1,128)} %bitcast.14, ...), custom_call_target="tpu_custom_call" | custom-call | tf_op jit(solution)/shard_map/pallas_call | solution.py:380
  77.7 2.3 %copy.13 = f32[64,32,128]{2,1,0:T(8,128)} copy(f32[64,32,128]{2,1,0:T(8,128)} %bitcast.8) | data formatting | bytes 2097152

commit v4 on v3

--- a/solution.py
+++ b/solution.py
@@ -126,9 +126,9 @@
 
 
     def attention(ring, line, whole, project, gate_bias, full, gated, sems, ready, send_home):
-        a, b, lane, index, device_of, mate = ring
+        a, b, last, index, device_of, mate = ring
         send_b, recv_b, send_c, recv_c = sems
-        others = (a + 1 - 2 * (a % 2), 3 - a, (a + 2) % 4)
+        others = ((a + 2) % 4, a + 1 - 2 * (a % 2), 3 - a)
         own, far = index(a, b), index(a, 1 - b)
 
         def bias_copy(place, send, device):
@@ -166,7 +166,7 @@
             pass_on(index(other, b))
 
         def chunk(t, carry):
-            half = (a // 2 + t + lane) % 2
+            half = (last + t + 1) % 2
             side = (b + t // 2) % 2
             pair = (index(2 * half, side), index(2 * half + 1, side))
             for place in pair:
@@ -248,18 +248,18 @@
             def _():
                 home_s[pl.ds(4 * c, 4)] = gated_s[:, pl.ds(pl.multiple_of(32 * c, 32), 32)]
 
-    ring_s = (x, y_lo, z, lambda a, b: 4 * b + a, lambda a: {"row": 4 * y_lo + a}, above)
+    ring_s = (x, y_lo, (z + z // 2 + 1 - y_lo) % 2, lambda a, b: 4 * b + a, lambda a: {"row": 4 * y_lo + a}, above)
     attention(
         ring_s, line_s, whole_s, project_s, gate_bias_s, full_s, gated_s,
         (send_b_s, recv_b_s, send_c_s, recv_c_s), ready_s, send_home_s,
     )
 
     weight_e = spread_weight(bias_e[...])
-    late_s = ((c // 4) % 2 + x // 2) % 2
     lane = lax.broadcasted_iota(jnp.int32, (32, 128), 1) % 32
 
     def residual(e, carry):
-        part = (late_s + e // 2) % 2 + 2 * (e % 2)
+        plane = z + (1 - e // 2) * (1 - 2 * (z % 2))
+        part = plane + (e % 2) * (3 - 2 * plane)
         for u in range(4):
             p = 4 * part + u
 
@@ -334,16 +334,14 @@
         def _():
             home_e[pl.ds(4 * r, 4)] = gated_e[:, pl.ds(pl.multiple_of(64 * r, 64), 64)]
 
-    ring_e = (z, y_hi, r // 2, lambda a, b: 2 * a + b, lambda a: {"col": 4 * a + 2 * y_hi + core}, across)
+    ring_e = (z, y_hi, y_lo, lambda a, b: 2 * a + b, lambda a: {"col": 4 * a + 2 * y_hi + core}, across)
     attention(
         ring_e, line_e, whole_e, project_e, gate_bias_e, full_e, gated_e,
         (send_b_e, recv_b_e, send_c_e, recv_c_e), ready_e, send_home_e,
     )
 
-    late_e = (y_lo + z // 2) % 2
-
     def finish(e, carry):
-        part = (late_e + e // 2) % 2 + 2 * (e % 2)
+        part = 2 * ((y_lo + 1 + e // 2) % 2) + e % 2
         for u in range(2):
             p = 2 * part + u
 

time: 80.1 us -> 78.3 us (0.978)
  Pallas kernels: 77.7 us -> 75.6 us
    pallas_call x1, Pallas kernels: 77.7 us -> 75.6 us  [local(): pl.pallas_call(kernel, out_shape=jax.ShapeDtypeStruct((2048, 128), F32),...]
where the time goes in v4:
time: 78.3 us; the launch traced here: 77.8 us
  Pallas kernels  75.6 us (97%)
  local copies, waits for them, and re-layouts  2.26 us (3%)
    pallas_call x1, Pallas kernels, local(): pl.pallas_call(kernel, out_shape=jax.ShapeDtypeStruct((2048, 128), F32),...  75.6 us
    unnamed x1, local copies, waits for them, and re-layouts  2.26 us

profile of v4, /device:TPU:16, one launch (start us, length us, event | category | flops | bytes accessed | tf_op | source)
XLA Modules:
  0.0 77.8 jit_solution(16730014470521944575)
XLA Ops:
  0.0 75.6 %shard_map.109 = f32[2048,128]{1,0:T(8,128)} custom-call(f32[2048,128]{1,0:T(8,128)} %bitcast.9, f32[1,128]{1,0:T(1,128)} %bitcast.12, bf16[128,512]{1,0:T(8,128)(2,1)} %project_s.1, f32[1,128]{1,0:T(1,128)} %bitcast.13, bf16[4,128]{1,0:T(4,128)(2,1)} %bitcast.10, bf16[128,128]{1,0:T(8,128)(2,1)} %out_s.1, f32[1,128]{1,0:T(1,128)} %bitcast.14, ...), custom_call_target="tpu_custom_call" | custom-call | tf_op jit(solution)/shard_map/pallas_call | solution.py:378
  75.6 2.3 %copy.13 = f32[64,32,128]{2,1,0:T(8,128)} copy(f32[64,32,128]{2,1,0:T(8,128)} %bitcast.8) | data formatting | bytes 2097152

commit v5 on v4

--- a/solution.py
+++ b/solution.py
@@ -110,7 +110,7 @@
     above = {"row": 4 * (1 - y_lo) + x, "col": 4 * z + 2 * ((y_hi + y_lo) % 2) + core}
 
     barrier = pltpu.get_barrier_semaphore()
-    for s in range(1, 16):
+    for s in (10, 11, 9, 6, 7, 5, 14, 15, 13, 8, 2, 3, 4, 12, 1):
         pl.semaphore_signal(barrier, inc=1, device_id={"col": (c + s) % 16}, device_id_type=MESH)
     for s in range(1, 8):
         pl.semaphore_signal(barrier, inc=1, device_id={"row": (r + s) % 8}, device_id_type=MESH)
@@ -165,25 +165,24 @@
         for other in others:
             pass_on(index(other, b))
 
-        def chunk(t, carry):
-            half = (last + t + 1) % 2
-            side = (b + t // 2) % 2
-            pair = (index(2 * half, side), index(2 * half + 1, side))
-            for place in pair:
+        def chunk(places):
+            for place in places:
                 from_sibling(place).wait_recv()
             for i in range(4):
-                attend(i, pair, full, query, key, value, gate, gated)
-            for place in pair:
+                attend(i, places, full, query, key, value, gate, gated)
+            for place in places:
                 send_home(place)
 
-            @pl.when(t == 1)
-            def _():
-                for other in others:
-                    pass_on(index(other, 1 - b))
-
+        chunk([index(k, b) for k in range(4)])
+        for other in others:
+            pass_on(index(other, 1 - b))
+
+        def far_chunk(t, carry):
+            half = (last + 1 + t) % 2
+            chunk([index(2 * half, 1 - b), index(2 * half + 1, 1 - b)])
             return carry
 
-        lax.fori_loop(0, 4, chunk, 0)
+        lax.fori_loop(0, 2, far_chunk, 0)
         bias_copy(own, 0, mate).wait_send()
         for k, other in enumerate(others):
             bias_copy(own, 1 + k, device_of(other)).wait_send()

time: 78.3 us -> 78.2 us (level)
  no operation moved by 1% of the time
where the time goes in v5:
time: 78.2 us; the launch traced here: 77.5 us
  Pallas kernels  75.3 us (96%)
  local copies, waits for them, and re-layouts  2.26 us (3%)
    pallas_call x1, Pallas kernels, local(): pl.pallas_call(kernel, out_shape=jax.ShapeDtypeStruct((2048, 128), F32),...  75.3 us
    unnamed x1, local copies, waits for them, and re-layouts  2.26 us

profile of v5, /device:TPU:16, one launch (start us, length us, event | category | flops | bytes accessed | tf_op | source)
XLA Modules:
  0.0 77.5 jit_solution(16701916050042031164)
XLA Ops:
  0.0 75.3 %shard_map.109 = f32[2048,128]{1,0:T(8,128)} custom-call(f32[2048,128]{1,0:T(8,128)} %bitcast.9, f32[1,128]{1,0:T(1,128)} %bitcast.12, bf16[128,512]{1,0:T(8,128)(2,1)} %project_s.1, f32[1,128]{1,0:T(1,128)} %bitcast.13, bf16[4,128]{1,0:T(4,128)(2,1)} %bitcast.10, bf16[128,128]{1,0:T(8,128)(2,1)} %out_s.1, f32[1,128]{1,0:T(1,128)} %bitcast.14, ...), custom_call_target="tpu_custom_call" | custom-call | tf_op jit(solution)/shard_map/pallas_call | solution.py:377
  75.3 2.3 %copy.13 = f32[64,32,128]{2,1,0:T(8,128)} copy(f32[64,32,128]{2,1,0:T(8,128)} %bitcast.8) | data formatting | bytes 2097152
